TPU v7x, 128 devices: a whole 4x4x4 slice. The times are simulated.
128 devices in a mesh: section: 2 (over core), expert: 16 (over z, y), head: 4 (over x).
Axes of the slice: x: 4, y: 4, z: 4, core: 2. Of those that a mesh axis runs over, the one named last changes fastest.
Arguments:
- inputs: bfloat16 [2, 2048, 768], P(None, 'expert'), may hold values from -6 to 6
- cotangent: bfloat16 [2, 2048, 768], P(None, 'expert'), may hold values from -6 to 6
- routes: int32 [2, 2, 2048, 2], P('section', None, 'expert'), may hold values from 0 to 31, all different within a row; in each aligned block of 128 rows (0 to 127, 128 to 255, ..., all dimensions but the last counted through in order) at most 12 rows name the same one
- attend_gain: bfloat16 [2, 768], P('section'), may hold values from 0.099609375 to 1.8984375
- query_key_value: bfloat16 [2, 3, 768, 768], P('section', None, None, 'head'), may hold values from -0.21875 to 0.21875
- attend_out: bfloat16 [2, 768, 768], P('section', 'head'), may hold values from -1.75 to 1.75
- position_bias: bfloat16 [2, 12, 32], P('section', 'head'), may hold values from -4 to 4
- mixture_gain: bfloat16 [2, 768], P('section'), may hold values from 0.099609375 to 1.8984375
- router: bfloat16 [2, 768, 32], P('section'), may hold values from -0.15625 to 0.15625
- expert_up: bfloat16 [2, 32, 768, 3072], P('section', 'expert', None, 'head'), may hold values from -0.21875 to 0.21875
- expert_down: bfloat16 [2, 32, 3072, 768], P('section', 'expert', 'head'), may hold values from -0.109375 to 0.109375
Outputs:
- section_output: bfloat16 [2, 2, 2048, 768], P('section', None, 'expert')
- input_grad: float32 [2, 2, 2048, 768], P('section', None, 'expert')
- grad_attend_gain: float32 [2, 768], P('section')
- grad_query_key_value: float32 [2, 3, 768, 768], P('section', None, None, 'head')
- grad_attend_out: float32 [2, 768, 768], P('section', 'head')
- grad_position_bias: float32 [2, 12, 32], P('section', 'head')
- grad_mixture_gain: float32 [2, 768], P('section')
- grad_router: float32 [2, 768, 32], P('section')
- grad_expert_up: float32 [2, 32, 768, 3072], P('section', 'expert', None, 'head')
- grad_expert_down: float32 [2, 32, 3072, 768], P('section', 'expert', 'head')
Inputs may be any that keep to these rules, and one draw needn't show every extreme that they name: `routes`: each token names two different experts. Among the 128 tokens of one sequence (one section, micro-batch and index of expert), no expert is named more than 12 times over both slots, and in every draw some expert is named exactly 12 times by some sequence.
All inputs are finite; a program needn't handle non-finite values.
Results may differ from a plain program's by a relative error of at most 0.028.
Values may be sent and summed in bfloat16 or wider, within the bound.
No kernel may reach another device: no remote copies, remote signals or barrier semaphores. Data moves between devices by JAX's collectives and lax.ppermute only.
A program may use at most 128 MiB of HBM per device.

v0:
```python
import jax
import jax.numpy as jnp
from jax import lax
from jax.sharding import PartitionSpec as P

HEAD_DIM = 64
EPS = 1e-06
NEG = -1e30


def passed_along(array, axis, by):
    length = lax.axis_size(axis)
    pairs = [(i, i + by) for i in range(length) if 0 <= i + by < length]
    return lax.ppermute(array, axis, pairs)


def norm_scale(values):
    return lax.rsqrt(jnp.mean(values * values, axis=-1, keepdims=True) + EPS)


def norm_back(grad_normed, values, scale, gain):
    unit = values * scale
    grad_gain = jnp.sum(grad_normed * unit, axis=0)
    grad_unit = grad_normed * gain
    grad_values = scale * (grad_unit - unit * jnp.mean(grad_unit * unit, axis=-1, keepdims=True))
    return (grad_values, grad_gain)


def position_tables(length, buckets):
    rows = lax.broadcasted_iota(jnp.int32, (length, length), 0)
    cols = lax.broadcasted_iota(jnp.int32, (length, length), 1)
    offset = rows - cols
    levels = lax.broadcasted_iota(jnp.int32, (buckets, length, length), 0)
    onehot = (jnp.clip(offset, 0, buckets - 1)[None] == levels).astype(jnp.bfloat16)
    return (offset >= 0, onehot)


def slot_targets(route_tile, experts, capacity):
    flat = route_tile.reshape(-1)
    levels = lax.broadcasted_iota(jnp.int32, (flat.shape[0], experts), 1)
    onehot = (flat[:, None] == levels).astype(jnp.int32)
    place = jnp.sum((jnp.cumsum(onehot, axis=0) - 1) * onehot, axis=1)
    return flat * capacity + place


def attend_scores(heads, table, causal, onehot):
    bias = jnp.einsum("bst,hb->hst", onehot, table, preferred_element_type=jnp.float32)
    scores = jnp.einsum("shd,thd->hst", heads[0], heads[1], preferred_element_type=jnp.float32)
    scores = scores * HEAD_DIM ** (-0.5) + bias
    return jnp.where(causal[None], scores, NEG)


def attend_forward(normed, proj_weight, out_weight, table, causal, onehot):
    length = normed.shape[0]
    local_heads = table.shape[0]
    projected = jnp.einsum(
        "sd,kde->kse", normed, proj_weight, preferred_element_type=jnp.float32
    ).astype(jnp.bfloat16)
    heads = projected.reshape(3, length, local_heads, HEAD_DIM)
    scores = attend_scores(heads, table, causal, onehot)
    top = jnp.max(scores, axis=-1, keepdims=True)
    weights = jnp.exp(scores - top)
    total = jnp.sum(weights, axis=-1, keepdims=True)
    probs = (weights / total).astype(jnp.bfloat16)
    mixed = jnp.einsum("hst,thd->shd", probs, heads[2], preferred_element_type=jnp.float32)
    mixed = mixed.reshape(length, local_heads * HEAD_DIM).astype(jnp.bfloat16)
    partial_out = jnp.dot(mixed, out_weight, preferred_element_type=jnp.float32)
    return (partial_out, (projected, mixed, top + jnp.log(total)))


def attend_backward(grad_attn, normed, proj_weight, out_weight, table, causal, onehot, saved_attn):
    projected, mixed, log_total = saved_attn
    length = normed.shape[0]
    local_heads = table.shape[0]
    heads = projected.reshape(3, length, local_heads, HEAD_DIM)
    grad_out_weight = jnp.einsum("se,sd->ed", mixed, grad_attn, preferred_element_type=jnp.float32)
    grad_mixed = jnp.einsum("sd,ed->se", grad_attn, out_weight, preferred_element_type=jnp.float32)
    grad_mixed = grad_mixed.astype(jnp.bfloat16).reshape(length, local_heads, HEAD_DIM)
    probs = jnp.exp(attend_scores(heads, table, causal, onehot) - log_total)
    grad_probs = jnp.einsum(
        "shd,thd->hst", grad_mixed, heads[2], preferred_element_type=jnp.float32
    )
    delta = jnp.sum(probs * grad_probs, axis=-1, keepdims=True)
    grad_scores = (probs * (grad_probs - delta)).astype(jnp.bfloat16)
    grad_table = jnp.einsum("bst,hst->hb", onehot, grad_scores, preferred_element_type=jnp.float32)
    factor = HEAD_DIM ** (-0.5)
    grad_query = (
        jnp.einsum("hst,thd->shd", grad_scores, heads[1], preferred_element_type=jnp.float32)
        * factor
    )
    grad_key = (
        jnp.einsum("hst,shd->thd", grad_scores, heads[0], preferred_element_type=jnp.float32)
        * factor
    )
    grad_value = jnp.einsum(
        "hst,shd->thd", probs.astype(jnp.bfloat16), grad_mixed, preferred_element_type=jnp.float32
    )
    grad_projected = (
        jnp.stack([grad_query, grad_key, grad_value])
        .reshape(3, length, local_heads * HEAD_DIM)
        .astype(jnp.bfloat16)
    )
    grad_proj_weight = jnp.einsum(
        "sd,kse->kde", normed, grad_projected, preferred_element_type=jnp.float32
    )
    grad_normed = jnp.einsum(
        "kse,kde->sd", grad_projected, proj_weight, preferred_element_type=jnp.float32
    )
    return (grad_normed, grad_proj_weight, grad_out_weight, grad_table)


def raise_hidden(arrived, up_weight):
    pre_act = jnp.einsum("erd,edf->erf", arrived, up_weight, preferred_element_type=jnp.float32)
    return (pre_act, jax.nn.gelu(pre_act).astype(jnp.bfloat16))


def gate_forward(logits, route_tile, experts):
    levels = lax.broadcasted_iota(jnp.int32, route_tile.shape + (experts,), 2)
    pick = (route_tile[:, :, None] == levels).astype(jnp.float32)
    chosen = jnp.sum(logits[:, None, :] * pick, axis=-1)
    top = jnp.max(chosen, axis=-1, keepdims=True)
    weights = jnp.exp(chosen - top)
    return (weights / jnp.sum(weights, axis=-1, keepdims=True), pick)


def layer_forward(layer_in, route_tile, params, tables):
    gain_a, proj_weight, out_weight, table, gain_m, router_weight, up_weight, down_weight = params
    causal, onehot = tables
    values = layer_in.astype(jnp.float32)
    length, width = values.shape
    experts = router_weight.shape[1]
    local_experts = up_weight.shape[0]
    capacity = 3 * length // experts
    scale_a = norm_scale(values)
    normed_a = (values * scale_a * gain_a).astype(jnp.bfloat16)
    partial_attn, saved_attn = attend_forward(
        normed_a, proj_weight, out_weight, table, causal, onehot
    )
    attended = lax.psum(partial_attn, "head")
    middle = values + attended
    scale_m = norm_scale(middle)
    normed_m = (middle * scale_m * gain_m).astype(jnp.bfloat16)
    logits = jnp.dot(normed_m, router_weight, preferred_element_type=jnp.float32)
    gates, pick = gate_forward(logits, route_tile, experts)
    target = slot_targets(route_tile, experts, capacity)
    buffer = (
        jnp.zeros((experts * capacity, width), jnp.bfloat16)
        .at[target]
        .set(jnp.repeat(normed_m, 2, axis=0))
    )
    arrived = lax.all_to_all(
        buffer.reshape(experts, 1, capacity, width),
        "expert",
        split_axis=0,
        concat_axis=1,
        tiled=True,
    )
    arrived = arrived.reshape(local_experts, -1, width)
    pre_act, hidden = raise_hidden(arrived, up_weight)
    partial_rows = jnp.einsum(
        "erf,efd->erd", hidden, down_weight, preferred_element_type=jnp.float32
    )
    returned = lax.all_to_all(
        partial_rows.reshape(local_experts, -1, capacity, width).astype(jnp.bfloat16),
        "expert",
        split_axis=1,
        concat_axis=0,
        tiled=True,
    ).astype(jnp.float32)
    slot_part = returned.reshape(experts * capacity, width)[target].reshape(length, 2, width)
    slot_out = lax.psum(slot_part.astype(jnp.bfloat16), "head").astype(jnp.float32)
    layer_out = middle + jnp.sum(gates[:, :, None] * slot_out, axis=1)
    owner_saved = (buffer,)
    saved = (
        values,
        scale_a,
        normed_a,
        saved_attn,
        middle,
        scale_m,
        normed_m,
        gates,
        pick,
        target,
        slot_out,
        owner_saved,
    )
    return (layer_out, saved)


def layer_backward(grad_out, saved, params, tables):
    gain_a, proj_weight, out_weight, table, gain_m, router_weight, up_weight, down_weight = params
    causal, onehot = tables
    (
        values,
        scale_a,
        normed_a,
        saved_attn,
        middle,
        scale_m,
        normed_m,
        gates,
        pick,
        target,
        slot_out,
        owner_saved,
    ) = saved
    length, width = values.shape
    experts = router_weight.shape[1]
    local_experts = up_weight.shape[0]
    capacity = 3 * length // experts
    grad_slots = (gates[:, :, None] * grad_out[:, None, :]).astype(jnp.bfloat16)
    grad_gates = jnp.sum(grad_out[:, None, :] * slot_out, axis=-1)
    grad_buffer = (
        jnp.zeros((experts * capacity, width), jnp.bfloat16)
        .at[target]
        .set(grad_slots.reshape(2 * length, width))
    )
    grad_buffer = grad_buffer.reshape(experts, 1, capacity, width)
    row_buffer = owner_saved[0].reshape(experts, 1, capacity, width)
    grad_arrived, arrived = (
        lax.all_to_all(grad_buffer, "expert", split_axis=0, concat_axis=1, tiled=True),
        lax.all_to_all(row_buffer, "expert", split_axis=0, concat_axis=1, tiled=True),
    )
    arrived = arrived.reshape(local_experts, -1, width)
    pre_act, hidden = raise_hidden(arrived, up_weight)
    grad_arrived = grad_arrived.reshape(local_experts, -1, width)
    grad_hidden = jnp.einsum(
        "erd,efd->erf", grad_arrived, down_weight, preferred_element_type=jnp.float32
    )
    unused, gelu_back = jax.vjp(jax.nn.gelu, pre_act)
    grad_pre = gelu_back(grad_hidden)[0].astype(jnp.bfloat16)
    grad_down = jnp.einsum("erf,erd->efd", hidden, grad_arrived, preferred_element_type=jnp.float32)
    grad_up = jnp.einsum("erd,erf->edf", arrived, grad_pre, preferred_element_type=jnp.float32)
    grad_rows = jnp.einsum("erf,edf->erd", grad_pre, up_weight, preferred_element_type=jnp.float32)
    returned = lax.all_to_all(
        grad_rows.reshape(local_experts, -1, capacity, width).astype(jnp.bfloat16),
        "expert",
        split_axis=1,
        concat_axis=0,
        tiled=True,
    ).astype(jnp.float32)
    grad_slot_rows = returned.reshape(experts * capacity, width)[target].reshape(length, 2, width)
    grad_normed_m = lax.psum(jnp.sum(grad_slot_rows, axis=1).astype(jnp.bfloat16), "head").astype(
        jnp.float32
    )
    grad_chosen = gates * (grad_gates - jnp.sum(gates * grad_gates, axis=-1, keepdims=True))
    grad_logits = jnp.sum(grad_chosen[:, :, None] * pick, axis=1).astype(jnp.bfloat16)
    grad_router = jnp.einsum("sd,se->de", normed_m, grad_logits, preferred_element_type=jnp.float32)
    grad_normed_m = grad_normed_m + jnp.einsum(
        "se,de->sd", grad_logits, router_weight, preferred_element_type=jnp.float32
    )
    grad_middle, grad_gain_m = norm_back(grad_normed_m, middle, scale_m, gain_m)
    grad_middle = grad_middle + grad_out
    grad_normed_a, grad_proj_weight, grad_out_weight, grad_table = attend_backward(
        grad_middle.astype(jnp.bfloat16),
        normed_a,
        proj_weight,
        out_weight,
        table,
        causal,
        onehot,
        saved_attn,
    )
    grad_normed_a = lax.psum(grad_normed_a.astype(jnp.bfloat16), "head").astype(jnp.float32)
    grad_values, grad_gain_a = norm_back(grad_normed_a, values, scale_a, gain_a)
    shared = (grad_gain_a, grad_proj_weight, grad_out_weight, grad_table, grad_gain_m, grad_router)
    return (grad_values + grad_middle, shared, (grad_up, grad_down))


def on_device(
    inputs,
    cotangent,
    routes,
    attend_gain,
    query_key_value,
    attend_out,
    position_bias,
    mixture_gain,
    router,
    expert_up,
    expert_down,
):
    micro = inputs.shape[0]
    length = inputs.shape[1]
    params = (
        attend_gain[0].astype(jnp.float32),
        query_key_value[0],
        attend_out[0],
        position_bias[0],
        mixture_gain[0].astype(jnp.float32),
        router[0],
        expert_up[0],
        expert_down[0],
    )
    tables = position_tables(length, position_bias.shape[2])
    first = lax.axis_index("section") == 0
    received = jnp.zeros((length, inputs.shape[2]), jnp.bfloat16)
    outputs = []
    caches = []
    for tick in range(micro + 1):
        layer_in = jnp.where(first, inputs[min(tick, micro - 1)], received)
        route_tile = jnp.where(first, routes[0, min(tick, micro - 1)], routes[0, max(tick - 1, 0)])
        layer_out, saved = layer_forward(layer_in, route_tile, params, tables)
        layer_low = layer_out.astype(jnp.bfloat16)
        outputs.append(layer_low)
        caches.append(saved)
        if tick < micro:
            received = passed_along(layer_low, "section", 1)
    section_output = jnp.stack(
        [jnp.where(first, outputs[index], outputs[index + 1]) for index in range(micro)]
    )[None]
    grad_received = jnp.zeros_like(received)
    shared_total = None
    owned_total = None
    grad_list = []
    for tick in range(micro + 1):
        late = cotangent[min(tick, micro - 1)].astype(jnp.float32)
        if tick == micro:
            late = jnp.zeros_like(late)
        grad_out = jnp.where(first, grad_received.astype(jnp.float32), late)
        saved = jax.tree.map(
            lambda early, later: jnp.where(first, early, later),
            caches[max(tick - 1, 0)],
            caches[min(tick + 1, micro)],
        )
        grad_in, shared, owned = layer_backward(grad_out, saved, params, tables)
        if shared_total is None:
            shared_total = shared
            owned_total = owned
        else:
            shared_total = jax.tree.map(lambda total, extra: total + extra, shared_total, shared)
            owned_total = jax.tree.map(lambda total, extra: total + extra, owned_total, owned)
        grad_list.append(grad_in)
        if tick < micro:
            grad_received = passed_along(grad_in.astype(jnp.bfloat16), "section", -1)
    gain_a, proj_part, out_part, table_part, gain_m, router_part = shared_total
    shared_total = (
        lax.psum(gain_a.astype(jnp.bfloat16), "expert").astype(jnp.float32),
        lax.psum(proj_part.astype(jnp.bfloat16), "expert").astype(jnp.float32),
        lax.psum(out_part.astype(jnp.bfloat16), "expert").astype(jnp.float32),
        lax.psum(table_part.astype(jnp.bfloat16), "expert").astype(jnp.float32),
        lax.psum(gain_m.astype(jnp.bfloat16), "expert").astype(jnp.float32),
        lax.psum(router_part.astype(jnp.bfloat16), "expert").astype(jnp.float32),
    )
    input_grad = jnp.stack(
        [jnp.where(first, grad_list[index + 1], grad_list[index]) for index in range(micro)]
    )[None]
    grad_gain_a, grad_proj, grad_out_weight, grad_table, grad_gain_m, grad_router = shared_total
    grad_up, grad_down = owned_total
    return (
        section_output,
        input_grad,
        grad_gain_a[None],
        grad_proj[None],
        grad_out_weight[None],
        grad_table[None],
        grad_gain_m[None],
        grad_router[None],
        grad_up[None],
        grad_down[None],
    )


def solution(mesh):
    return jax.shard_map(
        on_device,
        mesh=mesh,
        in_specs=(
            P(None, "expert", None),
            P(None, "expert", None),
            P("section", None, "expert", None),
            P("section", None),
            P("section", None, None, "head"),
            P("section", "head", None),
            P("section", "head", None),
            P("section", None),
            P("section", None, None),
            P("section", "expert", None, "head"),
            P("section", "expert", "head", None),
        ),
        out_specs=(
            P("section", None, "expert", None),
            P("section", None, "expert", None),
            P("section", None),
            P("section", None, None, "head"),
            P("section", "head", None),
            P("section", "head", None),
            P("section", None),
            P("section", None, None),
            P("section", "expert", None, "head"),
            P("section", "expert", "head", None),
        ),
        check_vma=False,
    )
```

profile of v0, /device:TPU:0, one launch (start us, length us, event | category | flops | bytes accessed | tf_op | source)
XLA Modules:
  0.0 950.1 jit_solution(12501314368429168360)
XLA Ops:
  22.1 39.1 %all-reduce.16.cloned.1.call-done = f32[128,768]{1,0:T(8,128)} async-done(((f32[128,768]{1,0:T(8,128)}), f32[128,768]{1,0:T(8,128)}) %all-reduce.16.cloned.1.call-update) | async-done | bytes 393232 | tf_op jit(solution)/shard_map/psum | solution.py:139
  68.0 19.2 %all_to_all.189 = bf16[32,1,12,768]{3,2,1,0:T(8,128)(2,1)S(1)} all-to-all(bf16[32,1,12,768]{3,2,1,0:T(8,128)(2,1)} %bitcast.600), channel_id=1, replica_groups=mesh['section'=2,'expert'=16,'head'=4] {'expert'}, dimensions={0} | all-to-all | bytes 1179648 | tf_op jit(solution)/shard_map/all_to_all | solution.py:151
  88.1 3.7 fusion.44
  94.4 3.6 all-to-all-start.1
  98.2 10.2 %all-to-all-done.1 = bf16[2,16,12,768]{3,0,2,1:T(2,128)(2,1)S(1)} async-done(((bf16[2,16,12,768]{3,0,2,1:T(2,128)(2,1)}), bf16[2,16,12,768]{3,0,2,1:T(2,128)(2,1)S(1)}, u32[]{:S(2)}, u32[]{:S(2)}) %all-to-all-start.1) | async-done | bytes 589856 | tf_op jit(solution)/shard_map/all_to_all | solution.py:163
  114.5 38.0 %all-reduce.18.cloned.1.call-done = bf16[128,2,768]{2,1,0:T(2,128)(2,1)} async-done(((bf16[128,2,768]{2,1,0:T(2,128)(2,1)}), bf16[128,2,768]{2,1,0:T(2,128)(2,1)}) %all-reduce.18.cloned.1.call-update) | async-done | bytes 393232 | tf_op jit(solution)/shard_map/psum | solution.py:171
  164.4 40.4 %all-reduce.20.cloned.1.call-done = f32[128,768]{1,0:T(8,128)} async-done(((f32[128,768]{1,0:T(8,128)}), f32[128,768]{1,0:T(8,128)}) %all-reduce.20.cloned.1.call-update) | async-done | bytes 393232 | tf_op jit(solution)/shard_map/psum | solution.py:139
  214.6 7.0 all-to-all-start.7
  225.1 8.9 all-to-all-done.7
  234.0 4.3 all-to-all-start.2
  244.1 5.9 all-to-all-done.2
  250.1 4.3 all-to-all-start.6
  259.3 3.8 fusion.47
  266.0 6.9 all-to-all-start.3
  284.2 5.0 all-to-all-start.8
  310.8 3.0 fusion.217
  313.8 3.1 fusion.176
  317.0 37.1 %all-reduce.36.cloned.1.call-done = (bf16[128,768]{1,0:T(8,128)(2,1)}, bf16[128,2,768]{2,1,0:T(2,128)(2,1)}) async-done(((bf16[128,768]{1,0:T(8,128)(2,1)}, bf16[128,2,768]{2,1,0:T(2,128)(2,1)}), (bf16[128,768]{1,0:T(8,128)(2,1)}, bf16[128,2,768]{2,1,0:T(2,128)(2,1)})) %all-reduce.36.cloned.1.call-update) | async-done | bytes 589840 | tf_op jit(solution)/shard_map/psum | solution.py:244
  354.1 4.0 fusion.170
  369.2 38.2 %all-reduce.24.cloned.1.call-done = bf16[128,768]{1,0:T(8,128)(2,1)} async-done(((bf16[128,768]{1,0:T(8,128)(2,1)}), bf16[128,768]{1,0:T(8,128)(2,1)}) %all-reduce.24.cloned.1.call-update) | async-done | bytes 196624 | tf_op jit(solution)/shard_map/psum | solution.py:265
  420.9 37.7 %all-reduce.22.cloned.1.call-done = f32[128,768]{1,0:T(8,128)} async-done(((f32[128,768]{1,0:T(8,128)}), f32[128,768]{1,0:T(8,128)}) %all-reduce.22.cloned.1.call-update) | async-done | bytes 393232 | tf_op jit(solution)/shard_map/psum | solution.py:139
  464.9 2.9 scatter_custom_fusion.2
  472.0 7.2 all-to-all-start.13
  486.3 5.2 all-to-all-done.13
  491.6 4.5 all-to-all-start.4
  504.0 6.3 all-to-all-done.4
  510.3 4.3 all-to-all-start.10
  520.0 7.7 all-to-all-done.10
  527.6 4.3 all-to-all-start.9
  538.2 2.9 fusion.50
  544.7 7.4 all-to-all-start.5
  562.6 4.8 all-to-all-start.11
  567.5 3.0 fusion.212
  591.9 3.1 fusion.177
  595.1 37.2 %all-reduce.34.cloned.1.call-done = (bf16[128,768]{1,0:T(8,128)(2,1)}, bf16[128,2,768]{2,1,0:T(2,128)(2,1)}) async-done(((bf16[128,768]{1,0:T(8,128)(2,1)}, bf16[128,2,768]{2,1,0:T(2,128)(2,1)}), (bf16[128,768]{1,0:T(8,128)(2,1)}, bf16[128,2,768]{2,1,0:T(2,128)(2,1)})) %all-reduce.34.cloned.1.call-update) | async-done | bytes 589840 | tf_op jit(solution)/shard_map/psum | solution.py:244
  649.4 39.0 %all-reduce.26.cloned.1.call-done = bf16[128,768]{1,0:T(8,128)(2,1)} async-done(((bf16[128,768]{1,0:T(8,128)(2,1)}), bf16[128,768]{1,0:T(8,128)(2,1)}) %all-reduce.26.cloned.1.call-update) | async-done | bytes 196624 | tf_op jit(solution)/shard_map/psum | solution.py:265
  707.3 7.2 all-to-all-start.12
  717.3 11.9 %all-to-all-done.12 = bf16[32,1,12,768]{3,2,1,0:T(8,128)(2,1)} async-done(((bf16[32,1,12,768]{3,2,1,0:T(8,128)(2,1)}), bf16[32,1,12,768]{3,2,1,0:T(8,128)(2,1)}, u32[]{:S(2)}, u32[]{:S(2)}) %all-to-all-start.12) | async-done | bytes 589856 | tf_op jit(solution)/shard_map/all_to_all | solution.py:222
  731.4 3.1 fusion.74
  736.9 4.2 all-to-all-start.14
  741.2 7.2 add_bitcast_fusion
  748.5 4.2 all-to-all-done.14
  762.5 7.3 add_bitcast_fusion.1
  769.7 30.9 %all-reduce.28.cloned.1.call-done = bf16[128,768]{1,0:T(8,128)(2,1)} async-done(((bf16[128,768]{1,0:T(8,128)(2,1)}), bf16[128,768]{1,0:T(8,128)(2,1)}) %all-reduce.28.cloned.1.call-update) | async-done | bytes 196624 | tf_op jit(solution)/shard_map/psum | solution.py:244
  806.6 3.5 fusion.34
  816.8 31.7 %all-reduce.30.cloned.1.call-done = bf16[128,768]{1,0:T(8,128)(2,1)} async-done(((bf16[128,768]{1,0:T(8,128)(2,1)}), bf16[128,768]{1,0:T(8,128)(2,1)}) %all-reduce.30.cloned.1.call-update) | async-done | bytes 196624 | tf_op jit(solution)/shard_map/psum | solution.py:265
  850.9 75.9 %all-reduce = (bf16[1,3,32]{2,1,0:T(4,128)(2,1)}, bf16[1,768]{1,0:T(2,128)(2,1)}, bf16[1,768]{1,0:T(2,128)(2,1)S(1)}, bf16[1,768,32]{1,2,0:T(8,128)(2,1)}) all-reduce(bf16[1,3,32]{2,1,0:T(4,128)(2,1)} %fusion.153, bf16[1,768]{1,0:T(2,128)(2,1)S(1)} %broadcast_in_dim.93, ...), channel_id=1, replica_groups=mesh['section'=2,'expert'=16,'head'=4] {'expert'}, use_global_device_ids=true, to_apply=%region_78.79 | all-reduce | flops 26208 | bytes 104832 | tf_op jit(solution)/shard_map/psum | solution.py:342
  934.2 6.0 all-reduce.32.cloned.1.call-done
  (777 shorter events, 276.6 us)
Async XLA Ops:
  7.2 80.9 %copy-start = (bf16[1,2,768,768]{3,2,1,0:T(8,128)(2,1)S(1)}, bf16[1,2,768,768]{3,2,1,0:T(8,128)(2,1)}, u32[]{:S(2)}) copy-start(bf16[1,2,768,768]{3,2,1,0:T(8,128)(2,1)} %param.20) | copy-start | bytes 7077892
  7.2 54.1 %all-reduce.16.cloned.1.call-start = ((), (), s32[]{:S(2)}) async-start(), calls=%async_computation.15 | async-start | bytes 786432 | tf_op jit(solution)/shard_map/psum | solution.py:139
  8.6 149.8 %copy-start.203 = (f32[128]{0:T(128)}, f32[128]{0:T(128)S(1)}, u32[]{:S(2)}) copy-start(f32[128]{0:T(128)S(1)} %fusion.245) | copy-start | bytes 1540
  9.3 149.7 %copy-start.103 = (f32[768]{0:T(1024)}, f32[768]{0:T(1024)S(1)}, u32[]{:S(2)}) copy-start(f32[768]{0:T(1024)S(1)} %convert_reduce_fusion.1) | copy-start | bytes 9220
  15.5 45.8 %copy-start.14 = (bf16[2,128,768]{2,1,0:T(8,128)(2,1)S(1)}, bf16[2,128,768]{2,1,0:T(8,128)(2,1)}, u32[]{:S(2)}) copy-start(bf16[2,128,768]{2,1,0:T(8,128)(2,1)} %param.11) | copy-start | bytes 1179652
  17.1 96.1 %copy-start.171 = (s32[128,2]{0,1:T(2,128)}, s32[128,2]{0,1:T(2,128)S(1)}, u32[]{:S(2)}) copy-start(s32[128,2]{0,1:T(2,128)S(1)} %get-tuple-element.130) | copy-start | bytes 3076
  20.6 185.8 %copy-start.119 = (f32[768]{0:T(1024)}, f32[768]{0:T(1024)S(1)}, u32[]{:S(2)}) copy-start(f32[768]{0:T(1024)S(1)} %convert_reduce_fusion) | copy-start | bytes 9220
  62.4 143.5 %copy-start.205 = (f32[128]{0:T(128)}, f32[128]{0:T(128)S(1)}, u32[]{:S(2)}) copy-start(f32[128]{0:T(128)S(1)} %multiply_reduce_fusion.8) | copy-start | bytes 1540
  94.4 14.0 %all-to-all-start.1 = ((bf16[2,16,12,768]{3,0,2,1:T(2,128)(2,1)}), bf16[2,16,12,768]{3,0,2,1:T(2,128)(2,1)S(1)}, u32[]{:S(2)}, u32[]{:S(2)}) async-start(bf16[2,16,12,768]{3,0,2,1:T(2,128)(2,1)} %bitcast.613), calls=%async_computation.1 | async-start | bytes 1179648 | tf_op jit(solution)/shard_map/all_to_all | solution.py:163
  97.9 54.5 %all-reduce.18.cloned.1.call-start = ((), (), s32[]{:S(2)}) async-start(), calls=%async_computation.16 | async-start | bytes 786432 | tf_op jit(solution)/shard_map/psum | solution.py:171
  113.2 91.6 %all-reduce.20.cloned.1.call-start = ((), (), s32[]{:S(2)}) async-start(), calls=%async_computation.17 | async-start | bytes 786432 | tf_op jit(solution)/shard_map/psum | solution.py:139
  114.5 44.6 %copy-start.9 = (bf16[1,3,768,192]{2,3,1,0:T(8,128)(2,1)S(1)}, bf16[1,3,768,192]{2,3,1,0:T(8,128)(2,1)}, u32[]{:S(2)}) copy-start(bf16[1,3,768,192]{2,3,1,0:T(8,128)(2,1)} %param.15) | copy-start | bytes 2654212
  155.7 2.5 collective-permute-start
  158.4 48.0 %copy-start.1 = (bf16[128,768]{1,0:T(8,128)(2,1)}, bf16[128,768]{1,0:T(8,128)(2,1)S(1)}, u32[]{:S(2)}) copy-start(bf16[128,768]{1,0:T(8,128)(2,1)S(1)} %get-tuple-element.96) | copy-start | bytes 589828
  214.6 19.4 %all-to-all-start.7 = ((bf16[32,1,12,768]{3,2,1,0:T(8,128)(2,1)}), bf16[32,1,12,768]{3,2,1,0:T(8,128)(2,1)}, u32[]{:S(2)}, u32[]{:S(2)}) async-start(bf16[32,1,12,768]{3,2,1,0:T(8,128)(2,1)} %bitcast.598), calls=%async_computation.7 | async-start | bytes 1572864 | tf_op jit(solution)/shard_map/all_to_all | solution.py:223
  234.0 16.1 %all-to-all-start.2 = ((bf16[32,1,12,768]{3,2,1,0:T(8,128)(2,1)}), bf16[32,1,12,768]{3,2,1,0:T(8,128)(2,1)}, u32[]{:S(2)}, u32[]{:S(2)}) async-start(bf16[32,1,12,768]{3,2,1,0:T(8,128)(2,1)} %bitcast.596), calls=%async_computation.2 | async-start | bytes 1572864 | tf_op jit(solution)/shard_map/all_to_all | solution.py:151
  250.1 15.9 %all-to-all-start.6 = ((bf16[32,1,12,768]{3,2,1,0:T(8,128)(2,1)}), bf16[32,1,12,768]{3,2,1,0:T(8,128)(2,1)}, u32[]{:S(2)}, u32[]{:S(2)}) async-start(bf16[32,1,12,768]{3,2,1,0:T(8,128)(2,1)} %bitcast.80), calls=%async_computation.6 | async-start | bytes 1572864 | tf_op jit(solution)/shard_map/all_to_all | solution.py:222
  266.0 17.4 %all-to-all-start.3 = ((bf16[2,16,12,768]{3,0,2,1:T(2,128)(2,1)}), bf16[2,16,12,768]{3,0,2,1:T(2,128)(2,1)S(1)}, u32[]{:S(2)}, u32[]{:S(2)}) async-start(bf16[2,16,12,768]{3,0,2,1:T(2,128)(2,1)} %bitcast.611), calls=%async_computation.3 | async-start | bytes 1179648 | tf_op jit(solution)/shard_map/all_to_all | solution.py:163
  284.2 15.4 %all-to-all-start.8 = ((bf16[2,16,12,768]{3,0,2,1:T(2,128)(2,1)}), bf16[2,16,12,768]{3,0,2,1:T(2,128)(2,1)S(1)}, u32[]{:S(2)}, u32[]{:S(2)}) async-start(bf16[2,16,12,768]{3,0,2,1:T(2,128)(2,1)} %bitcast.88), calls=%async_computation.8 | async-start | bytes 1179648 | tf_op jit(solution)/shard_map/all_to_all | solution.py:236
  289.1 64.9 %all-reduce.36.cloned.1.call-start = ((), (), s32[]{:S(2)}) async-start(), calls=%async_computation.25 | async-start | bytes 1179648 | tf_op jit(solution)/shard_map/psum | solution.py:244
  310.3 97.2 %all-reduce.24.cloned.1.call-start = ((), (), s32[]{:S(2)}) async-start(), calls=%async_computation.19 | async-start | bytes 393216 | tf_op jit(solution)/shard_map/psum | solution.py:265
  316.9 42.8 %copy-start.2 = (bf16[128,768]{1,0:T(8,128)(2,1)S(1)}, bf16[128,768]{1,0:T(8,128)(2,1)}, u32[]{:S(2)}) copy-start(bf16[128,768]{1,0:T(8,128)(2,1)} %copy-done.1) | copy-start | bytes 589828
  316.9 42.8 %copy-start.16 = (bf16[2,128,768]{2,1,0:T(8,128)(2,1)S(1)}, bf16[2,128,768]{2,1,0:T(8,128)(2,1)}, u32[]{:S(2)}) copy-start(bf16[2,128,768]{2,1,0:T(8,128)(2,1)} %param.11) | copy-start | bytes 1179652
  316.9 42.8 %copy-start.24 = (f32[128,768]{1,0:T(8,128)S(1)}, f32[128,768]{1,0:T(8,128)}, u32[]{:S(2)}) copy-start(f32[128,768]{1,0:T(8,128)} %all-reduce.16.cloned.1.call-done) | copy-start | bytes 1179652
  316.9 42.8 %copy-start.82 = (bf16[1,768,32]{1,2,0:T(8,128)(2,1)S(1)}, bf16[1,768,32]{1,2,0:T(8,128)(2,1)}, u32[]{:S(2)}) copy-start(bf16[1,768,32]{1,2,0:T(8,128)(2,1)} %param.19) | copy-start | bytes 147460
  316.9 42.8 %copy-start.120 = (f32[768]{0:T(1024)S(1)}, f32[768]{0:T(1024)}, u32[]{:S(2)}) copy-start(f32[768]{0:T(1024)} %copy-done.119) | copy-start | bytes 9220
  316.9 42.8 %copy-start.201 = (f32[128]{0:T(128)S(1)}, f32[128]{0:T(128)}, u32[]{:S(2)}) copy-start(f32[128]{0:T(128)} %get-tuple-element.144) | copy-start | bytes 1540
  365.2 93.4 %all-reduce.22.cloned.1.call-start = ((), (), s32[]{:S(2)}) async-start(), calls=%async_computation.18 | async-start | bytes 786432 | tf_op jit(solution)/shard_map/psum | solution.py:139
  367.3 42.1 %collective-permute-start.1 = (bf16[128,768]{1,0:T(8,128)(2,1)S(1)}, bf16[128,768]{1,0:T(8,128)(2,1)}, u32[]{:S(2)}, u32[]{:S(2)}) collective-permute-start(bf16[128,768]{1,0:T(8,128)(2,1)S(1)} %get-tuple-element.84), channel_id=1, source_target_pairs={{0,64},{1,65},{2,66},{3,67},{4,68},{5,69},{6,70},{7,71},{8,72},{9,... | collective-permute-start | bytes 589832 | tf_op jit(solution)/shard_map/ppermute | solution.py:14
  411.4 48.9 %copy-start.5 = (bf16[128,768]{1,0:T(8,128)(2,1)}, bf16[128,768]{1,0:T(8,128)(2,1)S(1)}, u32[]{:S(2)}) copy-start(bf16[128,768]{1,0:T(8,128)(2,1)S(1)} %get-tuple-element.92) | copy-start | bytes 589828
  472.0 19.5 %all-to-all-start.13 = ((bf16[32,1,12,768]{3,2,1,0:T(8,128)(2,1)}), bf16[32,1,12,768]{3,2,1,0:T(8,128)(2,1)}, u32[]{:S(2)}, u32[]{:S(2)}) async-start(bf16[32,1,12,768]{3,2,1,0:T(8,128)(2,1)} %bitcast.129), calls=%async_computation.13 | async-start | bytes 1572864 | tf_op jit(solution)/shard_map/all_to_all | solution.py:223
  481.3 16.1 %collective-permute-start.2 = (bf16[128,768]{1,0:T(8,128)(2,1)}, bf16[128,768]{1,0:T(8,128)(2,1)}, u32[]{:S(2)}, u32[]{:S(2)}) collective-permute-start(bf16[128,768]{1,0:T(8,128)(2,1)} %get-tuple-element.99), channel_id=1, source_target_pairs={{64,0},{65,1},{66,2},{67,3},{68,4},{69,5},{70,6},{71,7},{72,8},{73... | collective-permute-start | bytes 589832 | tf_op jit(solution)/shard_map/ppermute | solution.py:14
  491.6 18.7 %all-to-all-start.4 = ((bf16[32,1,12,768]{3,2,1,0:T(8,128)(2,1)}), bf16[32,1,12,768]{3,2,1,0:T(8,128)(2,1)}, u32[]{:S(2)}, u32[]{:S(2)}) async-start(bf16[32,1,12,768]{3,2,1,0:T(8,128)(2,1)} %bitcast.595), calls=%async_computation.4 | async-start | bytes 1572864 | tf_op jit(solution)/shard_map/all_to_all | solution.py:151
  510.3 17.3 %all-to-all-start.10 = ((bf16[32,1,12,768]{3,2,1,0:T(8,128)(2,1)}), bf16[32,1,12,768]{3,2,1,0:T(8,128)(2,1)}, u32[]{:S(2)}, u32[]{:S(2)}) async-start(bf16[32,1,12,768]{3,2,1,0:T(8,128)(2,1)} %bitcast.594), calls=%async_computation.10 | async-start | bytes 1572864 | tf_op jit(solution)/shard_map/all_to_all | solution.py:223
  527.6 17.1 %all-to-all-start.9 = ((bf16[32,1,12,768]{3,2,1,0:T(8,128)(2,1)}), bf16[32,1,12,768]{3,2,1,0:T(8,128)(2,1)}, u32[]{:S(2)}, u32[]{:S(2)}) async-start(bf16[32,1,12,768]{3,2,1,0:T(8,128)(2,1)} %bitcast.101), calls=%async_computation.9 | async-start | bytes 1572864 | tf_op jit(solution)/shard_map/all_to_all | solution.py:222
  544.7 17.9 %all-to-all-start.5 = ((bf16[2,16,12,768]{3,0,2,1:T(2,128)(2,1)}), bf16[2,16,12,768]{3,0,2,1:T(2,128)(2,1)}, u32[]{:S(2)}, u32[]{:S(2)}) async-start(bf16[2,16,12,768]{3,0,2,1:T(2,128)(2,1)} %bitcast.68), calls=%async_computation.5 | async-start | bytes 1179648 | tf_op jit(solution)/shard_map/all_to_all | solution.py:163
  562.6 15.4 %all-to-all-start.11 = ((bf16[2,16,12,768]{3,0,2,1:T(2,128)(2,1)}), bf16[2,16,12,768]{3,0,2,1:T(2,128)(2,1)}, u32[]{:S(2)}, u32[]{:S(2)}) async-start(bf16[2,16,12,768]{3,0,2,1:T(2,128)(2,1)} %bitcast.610), calls=%async_computation.11 | async-start | bytes 1179648 | tf_op jit(solution)/shard_map/all_to_all | solution.py:236
  567.4 64.8 %all-reduce.34.cloned.1.call-start = ((), (), s32[]{:S(2)}) async-start(), calls=%async_computation.24 | async-start | bytes 1179648 | tf_op jit(solution)/shard_map/psum | solution.py:244
  589.7 98.6 %all-reduce.26.cloned.1.call-start = ((), (), s32[]{:S(2)}) async-start(), calls=%async_computation.20 | async-start | bytes 393216 | tf_op jit(solution)/shard_map/psum | solution.py:265
  646.1 44.0 %copy-start.3 = (bf16[128,768]{1,0:T(8,128)(2,1)S(1)}, bf16[128,768]{1,0:T(8,128)(2,1)}, u32[]{:S(2)}) copy-start(bf16[128,768]{1,0:T(8,128)(2,1)} %copy-done.1) | copy-start | bytes 589828
  646.2 44.0 %copy-start.31 = (f32[128,768]{1,0:T(8,128)S(1)}, f32[128,768]{1,0:T(8,128)}, u32[]{:S(2)}) copy-start(f32[128,768]{1,0:T(8,128)} %copy-done.29) | copy-start | bytes 1179652
  693.2 3.3 collective-permute-start.3
  707.3 22.0 %all-to-all-start.12 = ((bf16[32,1,12,768]{3,2,1,0:T(8,128)(2,1)}), bf16[32,1,12,768]{3,2,1,0:T(8,128)(2,1)}, u32[]{:S(2)}, u32[]{:S(2)}) async-start(bf16[32,1,12,768]{3,2,1,0:T(8,128)(2,1)} %bitcast.597), calls=%async_computation.12 | async-start | bytes 1572864 | tf_op jit(solution)/shard_map/all_to_all | solution.py:222
  736.9 15.8 %all-to-all-start.14 = ((bf16[2,16,12,768]{3,0,2,1:T(2,128)(2,1)}), bf16[2,16,12,768]{3,0,2,1:T(2,128)(2,1)}, u32[]{:S(2)}, u32[]{:S(2)}) async-start(bf16[2,16,12,768]{3,0,2,1:T(2,128)(2,1)} %bitcast.612), calls=%async_computation.14 | async-start | bytes 1179648 | tf_op jit(solution)/shard_map/all_to_all | solution.py:236
  741.2 59.4 %all-reduce.28.cloned.1.call-start = ((), (), s32[]{:S(2)}) async-start(), calls=%async_computation.21 | async-start | bytes 393216 | tf_op jit(solution)/shard_map/psum | solution.py:244
  762.4 86.1 %all-reduce.30.cloned.1.call-start = ((), (), s32[]{:S(2)}) async-start(), calls=%async_computation.22 | async-start | bytes 393216 | tf_op jit(solution)/shard_map/psum | solution.py:265
  806.5 133.6 %all-reduce.32.cloned.1.call-start = ((), (), s32[]{:S(2)}) async-start(), calls=%async_computation.23 | async-start | bytes 2359296 | tf_op jit(solution)/shard_map/psum | solution.py:340
  811.1 121.0 %copy-start.65 = (f32[128,768]{1,0:T(8,128)S(1)}, f32[128,768]{1,0:T(8,128)}, u32[]{:S(2)}) copy-start(f32[128,768]{1,0:T(8,128)} %copy-done.64) | copy-start | bytes 1179652
  (204 other events, 1802.2 us)
Sparse Core Ops, SparseCore 0:
  16.6 44.6 all-reduce.15
  113.3 39.0 all-reduce.17
  162.0 42.7 all-reduce.19
  310.4 43.6 all-reduce.35
  365.3 42.0 all-reduce.23
  415.9 42.6 all-reduce.21
  589.8 42.4 all-reduce.33
  646.2 42.0 all-reduce.25
  762.5 38.0 all-reduce.27
  806.6 41.8 all-reduce.29
  852.5 87.6 all-reduce.31
where the time goes:
time: 963 us; the launch traced here: 950 us
  waiting for transfers between devices  445 us (46%)
  local copies, waits for them, and re-layouts  132 us (14%)
  matrix products  95.4 us (10%)
  blocking collectives  95.1 us (10%)
  other arithmetic  83 us (9%)
  starting transfers between devices  82.3 us (9%)
  between operations  17 us (2%)
    psum x3, waiting for transfers between devices, layer_forward(): attended = lax.psum(partial_attn, 'head')  117 us
    psum x3, waiting for transfers between devices, layer_backward(): lax.psum(grad_normed_a.astype(jnp.bfloat16), 'head').astype(jnp.float32)  109 us
    psum x3, waiting for transfers between devices, layer_backward(): lax.psum(jnp.sum(grad_slot_rows, axis=1).astype(jnp.bfloat16), 'head')  105 us
    psum x1, blocking collectives, on_device(): lax.psum(table_part.astype(jnp.bfloat16), 'expert').astype(jnp.float32)  75.9 us
    psum x1, waiting for transfers between devices, layer_forward(): lax.psum(slot_part.astype(jnp.bfloat16), 'head').astype(jnp.float32)  38 us
    all_to_all x3, waiting for transfers between devices, layer_backward(): lax.all_to_all(row_buffer, 'expert', split_axis=0, concat_axis=1, tiled=T...  21.8 us
  transfers between devices with their start and end apart: 29, of which 26 were waited for; matrix products, arithmetic and copies ran while one was open for 16% of the time, Pallas kernels for 0%

commit v1 on v0

--- a/solution.py
+++ b/solution.py
@@ -148,12 +148,18 @@
         .at[target]
         .set(jnp.repeat(normed_m, 2, axis=0))
     )
-    arrived = lax.all_to_all(
-        buffer.reshape(experts, 1, capacity, width),
-        "expert",
-        split_axis=0,
-        concat_axis=1,
-        tiled=True,
+    arrived = jnp.concatenate(
+        lax.all_to_all(
+            jnp.stack(
+                jnp.split(
+                    buffer.reshape(experts, 1, capacity, width), lax.axis_size("expert"), axis=0
+                )
+            ),
+            "expert",
+            0,
+            0,
+        ),
+        axis=1,
     )
     arrived = arrived.reshape(local_experts, -1, width)
     pre_act, hidden = raise_hidden(arrived, up_weight)

time: 963 us -> 990 us (1.028)
  local copies, waits for them, and re-layouts: 132 us -> 158 us
    another operation x5 -> x59, local copies, waits for them, and re-layouts: 0.38 us -> 23.2 us  [the longest x54 22.9 us: layer_forward(): jnp.stack(jnp.split(buffer.reshape(experts, 1, capacity, width), lax.axis...]
    unnamed x447 -> x536, local copies, waits for them, and re-layouts: 15.7 us -> 28 us
  transfers between devices with their start and end apart: 29 -> 29, of which waited for: 26 -> 27; matrix products, arithmetic and copies ran while one was open for 16% -> 17% of each run, Pallas kernels for 0% -> 0%
where the time goes in v1:
time: 990 us; the launch traced here: 976 us
  waiting for transfers between devices  449 us (45%)
  local copies, waits for them, and re-layouts  158 us (16%)
  matrix products  97 us (10%)
  blocking collectives  93.3 us (9%)
  other arithmetic  81.4 us (8%)
  starting transfers between devices  79.4 us (8%)
  between operations  17.8 us (2%)
    psum x3, waiting for transfers between devices, layer_forward(): attended = lax.psum(partial_attn, 'head')  121 us
    psum x3, waiting for transfers between devices, layer_backward(): lax.psum(grad_normed_a.astype(jnp.bfloat16), 'head').astype(jnp.float32)  111 us
    psum x3, waiting for transfers between devices, layer_backward(): lax.psum(jnp.sum(grad_slot_rows, axis=1).astype(jnp.bfloat16), 'head')  106 us
    psum x1, blocking collectives, on_device(): lax.psum(table_part.astype(jnp.bfloat16), 'expert').astype(jnp.float32)  76 us
    psum x1, waiting for transfers between devices, layer_forward(): lax.psum(slot_part.astype(jnp.bfloat16), 'head').astype(jnp.float32)  37.6 us
    unnamed x536, local copies, waits for them, and re-layouts  28 us
    another operation x54, local copies, waits for them, and re-layouts, layer_forward(): jnp.stack(jnp.split(buffer.reshape(experts, 1, capacity, width), lax.axis...  22.9 us
    all_to_all x3, waiting for transfers between devices, layer_backward(): lax.all_to_all(row_buffer, 'expert', split_axis=0, concat_axis=1, tiled=T...  21 us
  transfers between devices with their start and end apart: 29, of which 27 were waited for; matrix products, arithmetic and copies ran while one was open for 17% of the time, Pallas kernels for 0%

profile of v1, /device:TPU:0, one launch (start us, length us, event | category | flops | bytes accessed | tf_op | source)
XLA Modules:
  0.0 976.0 jit_solution(983627649566766016)
XLA Ops:
  22.2 39.2 %all-reduce.16.cloned.1.call-done = f32[128,768]{1,0:T(8,128)} async-done(((f32[128,768]{1,0:T(8,128)}), f32[128,768]{1,0:T(8,128)}) %all-reduce.16.cloned.1.call-update) | async-done | bytes 393232 | tf_op jit(solution)/shard_map/psum | solution.py:139
  85.5 17.3 %all_to_all.159 = bf16[16,2,1,12,768]{4,1,3,2,0:T(2,128)(2,1)S(1)} all-to-all(bf16[16,2,1,12,768]{4,1,3,2,0:T(2,128)(2,1)S(1)} %copy.224), channel_id=1, replica_groups=mesh['section'=2,'expert'=16,'head'=4] {'expert'}, dimensions={0} | all-to-all | bytes 1179648 | tf_op jit(solution)/shard_map/all_to_all | solution.py:152
  102.8 3.8 fusion.44
  109.1 3.6 all-to-all-start.1
  113.4 9.7 all-to-all-done.1
  129.3 37.6 %all-reduce.18.cloned.1.call-done = bf16[128,2,768]{2,1,0:T(2,128)(2,1)} async-done(((bf16[128,2,768]{2,1,0:T(2,128)(2,1)}), bf16[128,2,768]{2,1,0:T(2,128)(2,1)}) %all-reduce.18.cloned.1.call-update) | async-done | bytes 393232 | tf_op jit(solution)/shard_map/psum | solution.py:177
  180.3 39.2 %all-reduce.20.cloned.1.call-done = f32[128,768]{1,0:T(8,128)} async-done(((f32[128,768]{1,0:T(8,128)}), f32[128,768]{1,0:T(8,128)}) %all-reduce.20.cloned.1.call-update) | async-done | bytes 393232 | tf_op jit(solution)/shard_map/psum | solution.py:139
  229.7 7.2 all-to-all-start.7
  238.9 10.3 %all-to-all-done.7 = bf16[32,1,12,768]{3,2,1,0:T(8,128)(2,1)} async-done(((bf16[32,1,12,768]{3,2,1,0:T(8,128)(2,1)}), bf16[32,1,12,768]{3,2,1,0:T(8,128)(2,1)}, u32[]{:S(2)}, u32[]{:S(2)}) %all-to-all-start.7) | async-done | bytes 589856 | tf_op jit(solution)/shard_map/all_to_all | solution.py:229
  249.2 4.2 all-to-all-start.2
  259.3 4.7 all-to-all-done.2
  264.0 4.3 all-to-all-start.6
  271.0 3.3 fusion.47
  275.7 4.2 all-to-all-done.6
  279.9 3.8 all-to-all-start.3
  295.0 4.9 all-to-all-start.8
  321.5 3.0 fusion.217
  324.6 3.1 fusion.176
  327.7 37.1 %all-reduce.36.cloned.1.call-done = (bf16[128,768]{1,0:T(8,128)(2,1)}, bf16[128,2,768]{2,1,0:T(2,128)(2,1)}) async-done(((bf16[128,768]{1,0:T(8,128)(2,1)}, bf16[128,2,768]{2,1,0:T(2,128)(2,1)}), (bf16[128,768]{1,0:T(8,128)(2,1)}, bf16[128,2,768]{2,1,0:T(2,128)(2,1)})) %all-reduce.36.cloned.1.call-update) | async-done | bytes 589840 | tf_op jit(solution)/shard_map/psum | solution.py:250
  364.8 4.0 fusion.170
  387.7 40.5 %all-reduce.24.cloned.1.call-done = bf16[128,768]{1,0:T(8,128)(2,1)} async-done(((bf16[128,768]{1,0:T(8,128)(2,1)}), bf16[128,768]{1,0:T(8,128)(2,1)}) %all-reduce.24.cloned.1.call-update) | async-done | bytes 196624 | tf_op jit(solution)/shard_map/psum | solution.py:271
  439.2 42.4 %all-reduce.22.cloned.1.call-done = f32[128,768]{1,0:T(8,128)} async-done(((f32[128,768]{1,0:T(8,128)}), f32[128,768]{1,0:T(8,128)}) %all-reduce.22.cloned.1.call-update) | async-done | bytes 393232 | tf_op jit(solution)/shard_map/psum | solution.py:139
  488.0 2.9 scatter_custom_fusion.2
  503.1 7.0 all-to-all-start.13
  517.9 4.5 all-to-all-done.13
  522.4 4.4 all-to-all-start.4
  537.4 6.5 all-to-all-start.10
  549.3 6.2 all-to-all-done.10
  555.5 4.3 all-to-all-start.9
  562.9 3.1 fusion.50
  571.4 5.3 all-to-all-start.5
  587.2 4.7 all-to-all-start.11
  592.2 3.1 fusion.212
  615.9 3.1 fusion.177
  619.1 38.2 %all-reduce.34.cloned.1.call-done = (bf16[128,768]{1,0:T(8,128)(2,1)}, bf16[128,2,768]{2,1,0:T(2,128)(2,1)}) async-done(((bf16[128,768]{1,0:T(8,128)(2,1)}, bf16[128,2,768]{2,1,0:T(2,128)(2,1)}), (bf16[128,768]{1,0:T(8,128)(2,1)}, bf16[128,2,768]{2,1,0:T(2,128)(2,1)})) %all-reduce.34.cloned.1.call-update) | async-done | bytes 589840 | tf_op jit(solution)/shard_map/psum | solution.py:250
  674.4 39.0 %all-reduce.26.cloned.1.call-done = bf16[128,768]{1,0:T(8,128)(2,1)} async-done(((bf16[128,768]{1,0:T(8,128)(2,1)}), bf16[128,768]{1,0:T(8,128)(2,1)}) %all-reduce.26.cloned.1.call-update) | async-done | bytes 196624 | tf_op jit(solution)/shard_map/psum | solution.py:271
  732.3 7.0 all-to-all-start.12
  742.2 12.5 %all-to-all-done.12 = bf16[32,1,12,768]{3,2,1,0:T(8,128)(2,1)} async-done(((bf16[32,1,12,768]{3,2,1,0:T(8,128)(2,1)}), bf16[32,1,12,768]{3,2,1,0:T(8,128)(2,1)}, u32[]{:S(2)}, u32[]{:S(2)}) %all-to-all-start.12) | async-done | bytes 589856 | tf_op jit(solution)/shard_map/all_to_all | solution.py:228
  756.9 3.1 fusion.74
  762.4 4.2 all-to-all-start.14
  766.9 7.2 add_bitcast_fusion
  774.1 4.4 all-to-all-done.14
  788.3 7.3 add_bitcast_fusion.1
  795.5 30.9 %all-reduce.28.cloned.1.call-done = bf16[128,768]{1,0:T(8,128)(2,1)} async-done(((bf16[128,768]{1,0:T(8,128)(2,1)}), bf16[128,768]{1,0:T(8,128)(2,1)}) %all-reduce.28.cloned.1.call-update) | async-done | bytes 196624 | tf_op jit(solution)/shard_map/psum | solution.py:250
  832.4 3.5 fusion.34
  842.6 31.7 %all-reduce.30.cloned.1.call-done = bf16[128,768]{1,0:T(8,128)(2,1)} async-done(((bf16[128,768]{1,0:T(8,128)(2,1)}), bf16[128,768]{1,0:T(8,128)(2,1)}) %all-reduce.30.cloned.1.call-update) | async-done | bytes 196624 | tf_op jit(solution)/shard_map/psum | solution.py:271
  876.7 76.0 %all-reduce = (bf16[1,3,32]{2,1,0:T(4,128)(2,1)}, bf16[1,768]{1,0:T(2,128)(2,1)}, bf16[1,768]{1,0:T(2,128)(2,1)S(1)}, bf16[1,768,32]{1,2,0:T(8,128)(2,1)}) all-reduce(bf16[1,3,32]{2,1,0:T(4,128)(2,1)} %fusion.153, bf16[1,768]{1,0:T(2,128)(2,1)S(1)} %broadcast_in_dim.93, ...), channel_id=1, replica_groups=mesh['section'=2,'expert'=16,'head'=4] {'expert'}, use_global_device_ids=true, to_apply=%region_78.79 | all-reduce | flops 26208 | bytes 104832 | tf_op jit(solution)/shard_map/psum | solution.py:348
  960.0 6.0 all-reduce.32.cloned.1.call-done
  (912 shorter events, 304.9 us)
Async XLA Ops:
  7.2 95.6 %copy-start = (bf16[1,2,768,768]{3,2,1,0:T(8,128)(2,1)S(1)}, bf16[1,2,768,768]{3,2,1,0:T(8,128)(2,1)}, u32[]{:S(2)}) copy-start(bf16[1,2,768,768]{3,2,1,0:T(8,128)(2,1)} %param.20) | copy-start | bytes 7077892
  7.2 54.1 %all-reduce.16.cloned.1.call-start = ((), (), s32[]{:S(2)}) async-start(), calls=%async_computation.15 | async-start | bytes 786432 | tf_op jit(solution)/shard_map/psum | solution.py:139
  9.3 164.2 %copy-start.109 = (f32[768]{0:T(1024)}, f32[768]{0:T(1024)S(1)}, u32[]{:S(2)}) copy-start(f32[768]{0:T(1024)S(1)} %convert_reduce_fusion.1) | copy-start | bytes 9220
  15.5 45.8 %copy-start.14 = (bf16[2,128,768]{2,1,0:T(8,128)(2,1)S(1)}, bf16[2,128,768]{2,1,0:T(8,128)(2,1)}, u32[]{:S(2)}) copy-start(bf16[2,128,768]{2,1,0:T(8,128)(2,1)} %param.11) | copy-start | bytes 1179652
  17.1 110.8 %copy-start.190 = (s32[128,2]{0,1:T(2,128)}, s32[128,2]{0,1:T(2,128)S(1)}, u32[]{:S(2)}) copy-start(s32[128,2]{0,1:T(2,128)S(1)} %get-tuple-element.178) | copy-start | bytes 3076
  20.6 200.5 %copy-start.121 = (f32[768]{0:T(1024)}, f32[768]{0:T(1024)S(1)}, u32[]{:S(2)}) copy-start(f32[768]{0:T(1024)S(1)} %convert_reduce_fusion) | copy-start | bytes 9220
  63.6 49.7 %copy-start.61 = (bf16[128,768]{1,0:T(8,128)(2,1)}, bf16[128,768]{1,0:T(8,128)(2,1)S(1)}, u32[]{:S(2)}) copy-start(bf16[128,768]{1,0:T(8,128)(2,1)S(1)} %multiply_convert_fusion.14) | copy-start | bytes 589828
  109.1 14.0 %all-to-all-start.1 = ((bf16[2,16,12,768]{3,0,2,1:T(2,128)(2,1)}), bf16[2,16,12,768]{3,0,2,1:T(2,128)(2,1)S(1)}, u32[]{:S(2)}, u32[]{:S(2)}) async-start(bf16[2,16,12,768]{3,0,2,1:T(2,128)(2,1)} %bitcast.602), calls=%async_computation.1 | async-start | bytes 1179648 | tf_op jit(solution)/shard_map/all_to_all | solution.py:169
  112.7 54.3 %all-reduce.18.cloned.1.call-start = ((), (), s32[]{:S(2)}) async-start(), calls=%async_computation.16 | async-start | bytes 786432 | tf_op jit(solution)/shard_map/psum | solution.py:177
  127.9 91.6 %all-reduce.20.cloned.1.call-start = ((), (), s32[]{:S(2)}) async-start(), calls=%async_computation.17 | async-start | bytes 786432 | tf_op jit(solution)/shard_map/psum | solution.py:139
  129.3 43.6 %copy-start.222 = (f32[128]{0:T(128)S(1)}, f32[128]{0:T(128)}, u32[]{:S(2)}) copy-start(f32[128]{0:T(128)} %copy-done.221) | copy-start | bytes 1540
  129.3 44.2 %copy-start.9 = (bf16[1,3,768,192]{2,3,1,0:T(8,128)(2,1)S(1)}, bf16[1,3,768,192]{2,3,1,0:T(8,128)(2,1)}, u32[]{:S(2)}) copy-start(bf16[1,3,768,192]{2,3,1,0:T(8,128)(2,1)} %param.15) | copy-start | bytes 2654212
  170.2 2.5 collective-permute-start
  172.8 48.3 %copy-start.1 = (bf16[128,768]{1,0:T(8,128)(2,1)}, bf16[128,768]{1,0:T(8,128)(2,1)S(1)}, u32[]{:S(2)}) copy-start(bf16[128,768]{1,0:T(8,128)(2,1)S(1)} %get-tuple-element.96) | copy-start | bytes 589828
  177.7 42.9 %copy-start.225 = (f32[128]{0:T(128)S(1)}, f32[128]{0:T(128)}, u32[]{:S(2)}) copy-start(f32[128]{0:T(128)} %copy-done.224) | copy-start | bytes 1540
  229.7 19.5 %all-to-all-start.7 = ((bf16[32,1,12,768]{3,2,1,0:T(8,128)(2,1)}), bf16[32,1,12,768]{3,2,1,0:T(8,128)(2,1)}, u32[]{:S(2)}, u32[]{:S(2)}) async-start(bf16[32,1,12,768]{3,2,1,0:T(8,128)(2,1)} %bitcast.586), calls=%async_computation.7 | async-start | bytes 1572864 | tf_op jit(solution)/shard_map/all_to_all | solution.py:229
  249.2 14.8 %all-to-all-start.2 = ((bf16[16,2,1,12,768]{4,1,3,2,0:T(2,128)(2,1)}), bf16[16,2,1,12,768]{4,1,3,2,0:T(2,128)(2,1)}, u32[]{:S(2)}, u32[]{:S(2)}) async-start(bf16[16,2,1,12,768]{4,1,3,2,0:T(2,128)(2,1)} %copy.234), calls=%async_computation.2 | async-start | bytes 1179648 | tf_op jit(solution)/shard_map/all_to_all | solution.py:152
  264.0 15.9 %all-to-all-start.6 = ((bf16[32,1,12,768]{3,2,1,0:T(8,128)(2,1)}), bf16[32,1,12,768]{3,2,1,0:T(8,128)(2,1)}, u32[]{:S(2)}, u32[]{:S(2)}) async-start(bf16[32,1,12,768]{3,2,1,0:T(8,128)(2,1)} %bitcast.74), calls=%async_computation.6 | async-start | bytes 1572864 | tf_op jit(solution)/shard_map/all_to_all | solution.py:228
  279.9 14.3 %all-to-all-start.3 = ((bf16[2,16,12,768]{3,0,2,1:T(2,128)(2,1)}), bf16[2,16,12,768]{3,0,2,1:T(2,128)(2,1)S(1)}, u32[]{:S(2)}, u32[]{:S(2)}) async-start(bf16[2,16,12,768]{3,0,2,1:T(2,128)(2,1)} %bitcast.601), calls=%async_computation.3 | async-start | bytes 1179648 | tf_op jit(solution)/shard_map/all_to_all | solution.py:169
  295.0 15.4 %all-to-all-start.8 = ((bf16[2,16,12,768]{3,0,2,1:T(2,128)(2,1)}), bf16[2,16,12,768]{3,0,2,1:T(2,128)(2,1)S(1)}, u32[]{:S(2)}, u32[]{:S(2)}) async-start(bf16[2,16,12,768]{3,0,2,1:T(2,128)(2,1)} %bitcast.82), calls=%async_computation.8 | async-start | bytes 1179648 | tf_op jit(solution)/shard_map/all_to_all | solution.py:242
  299.9 64.9 %all-reduce.36.cloned.1.call-start = ((), (), s32[]{:S(2)}) async-start(), calls=%async_computation.25 | async-start | bytes 1179648 | tf_op jit(solution)/shard_map/psum | solution.py:250
  321.0 107.2 %all-reduce.24.cloned.1.call-start = ((), (), s32[]{:S(2)}) async-start(), calls=%async_computation.19 | async-start | bytes 393216 | tf_op jit(solution)/shard_map/psum | solution.py:271
  380.7 47.5 %copy-start.17 = (bf16[2,128,768]{2,1,0:T(8,128)(2,1)S(1)}, bf16[2,128,768]{2,1,0:T(8,128)(2,1)}, u32[]{:S(2)}) copy-start(bf16[2,128,768]{2,1,0:T(8,128)(2,1)} %param.11) | copy-start | bytes 1179652
  382.7 47.4 %copy-start.33 = (f32[128,768]{1,0:T(8,128)S(1)}, f32[128,768]{1,0:T(8,128)}, u32[]{:S(2)}) copy-start(f32[128,768]{1,0:T(8,128)} %copy-done.32) | copy-start | bytes 1179652
  382.7 47.4 %collective-permute-start.1 = (bf16[128,768]{1,0:T(8,128)(2,1)}, bf16[128,768]{1,0:T(8,128)(2,1)}, u32[]{:S(2)}, u32[]{:S(2)}) collective-permute-start(bf16[128,768]{1,0:T(8,128)(2,1)} %get-tuple-element.84), channel_id=1, source_target_pairs={{0,64},{1,65},{2,66},{3,67},{4,68},{5,69},{6,70},{7,71},{8,72},{9,... | collective-permute-start | bytes 589832 | tf_op jit(solution)/shard_map/ppermute | solution.py:14
  385.9 95.7 %all-reduce.22.cloned.1.call-start = ((), (), s32[]{:S(2)}) async-start(), calls=%async_computation.18 | async-start | bytes 786432 | tf_op jit(solution)/shard_map/psum | solution.py:139
  432.0 51.4 %copy-start.5 = (bf16[128,768]{1,0:T(8,128)(2,1)}, bf16[128,768]{1,0:T(8,128)(2,1)S(1)}, u32[]{:S(2)}) copy-start(bf16[128,768]{1,0:T(8,128)(2,1)S(1)} %get-tuple-element.92) | copy-start | bytes 589828
  432.7 97.2 %collective-permute-start.2 = (bf16[128,768]{1,0:T(8,128)(2,1)}, bf16[128,768]{1,0:T(8,128)(2,1)}, u32[]{:S(2)}, u32[]{:S(2)}) collective-permute-start(bf16[128,768]{1,0:T(8,128)(2,1)} %get-tuple-element.147), channel_id=1, source_target_pairs={{64,0},{65,1},{66,2},{67,3},{68,4},{69,5},{70,6},{71,7},{72,8},{73... | collective-permute-start | bytes 589832 | tf_op jit(solution)/shard_map/ppermute | solution.py:14
  437.4 45.3 %copy-start.226 = (f32[128]{0:T(128)S(1)}, f32[128]{0:T(128)}, u32[]{:S(2)}) copy-start(f32[128]{0:T(128)} %copy-done.224) | copy-start | bytes 1540
  437.4 45.3 %copy-start.230 = (f32[128]{0:T(128)S(1)}, f32[128]{0:T(128)}, u32[]{:S(2)}) copy-start(f32[128]{0:T(128)} %copy-done.229) | copy-start | bytes 1540
  437.4 45.9 %copy-start.123 = (f32[768]{0:T(1024)S(1)}, f32[768]{0:T(1024)}, u32[]{:S(2)}) copy-start(f32[768]{0:T(1024)} %copy-done.121) | copy-start | bytes 9220
  503.1 19.3 %all-to-all-start.13 = ((bf16[32,1,12,768]{3,2,1,0:T(8,128)(2,1)}), bf16[32,1,12,768]{3,2,1,0:T(8,128)(2,1)S(1)}, u32[]{:S(2)}, u32[]{:S(2)}) async-start(bf16[32,1,12,768]{3,2,1,0:T(8,128)(2,1)} %bitcast.587), calls=%async_computation.13 | async-start | bytes 1572864 | tf_op jit(solution)/shard_map/all_to_all | solution.py:229
  522.4 14.9 %all-to-all-start.4 = ((bf16[16,2,1,12,768]{4,1,3,2,0:T(2,128)(2,1)}), bf16[16,2,1,12,768]{4,1,3,2,0:T(2,128)(2,1)}, u32[]{:S(2)}, u32[]{:S(2)}) async-start(bf16[16,2,1,12,768]{4,1,3,2,0:T(2,128)(2,1)} %copy.242), calls=%async_computation.4 | async-start | bytes 1179648 | tf_op jit(solution)/shard_map/all_to_all | solution.py:152
  537.4 18.1 %all-to-all-start.10 = ((bf16[32,1,12,768]{3,2,1,0:T(8,128)(2,1)}), bf16[32,1,12,768]{3,2,1,0:T(8,128)(2,1)}, u32[]{:S(2)}, u32[]{:S(2)}) async-start(bf16[32,1,12,768]{3,2,1,0:T(8,128)(2,1)} %bitcast.588), calls=%async_computation.10 | async-start | bytes 1572864 | tf_op jit(solution)/shard_map/all_to_all | solution.py:229
  555.5 15.9 %all-to-all-start.9 = ((bf16[32,1,12,768]{3,2,1,0:T(8,128)(2,1)}), bf16[32,1,12,768]{3,2,1,0:T(8,128)(2,1)}, u32[]{:S(2)}, u32[]{:S(2)}) async-start(bf16[32,1,12,768]{3,2,1,0:T(8,128)(2,1)} %bitcast.589), calls=%async_computation.9 | async-start | bytes 1572864 | tf_op jit(solution)/shard_map/all_to_all | solution.py:228
  571.4 15.8 %all-to-all-start.5 = ((bf16[2,16,12,768]{3,0,2,1:T(2,128)(2,1)}), bf16[2,16,12,768]{3,0,2,1:T(2,128)(2,1)}, u32[]{:S(2)}, u32[]{:S(2)}) async-start(bf16[2,16,12,768]{3,0,2,1:T(2,128)(2,1)} %bitcast.62), calls=%async_computation.5 | async-start | bytes 1179648 | tf_op jit(solution)/shard_map/all_to_all | solution.py:169
  587.2 15.2 %all-to-all-start.11 = ((bf16[2,16,12,768]{3,0,2,1:T(2,128)(2,1)}), bf16[2,16,12,768]{3,0,2,1:T(2,128)(2,1)}, u32[]{:S(2)}, u32[]{:S(2)}) async-start(bf16[2,16,12,768]{3,0,2,1:T(2,128)(2,1)} %bitcast.600), calls=%async_computation.11 | async-start | bytes 1179648 | tf_op jit(solution)/shard_map/all_to_all | solution.py:242
  591.9 65.4 %all-reduce.34.cloned.1.call-start = ((), (), s32[]{:S(2)}) async-start(), calls=%async_computation.24 | async-start | bytes 1179648 | tf_op jit(solution)/shard_map/psum | solution.py:250
  614.2 99.2 %all-reduce.26.cloned.1.call-start = ((), (), s32[]{:S(2)}) async-start(), calls=%async_computation.20 | async-start | bytes 393216 | tf_op jit(solution)/shard_map/psum | solution.py:271
  671.2 44.0 %copy-start.3 = (bf16[128,768]{1,0:T(8,128)(2,1)S(1)}, bf16[128,768]{1,0:T(8,128)(2,1)}, u32[]{:S(2)}) copy-start(bf16[128,768]{1,0:T(8,128)(2,1)} %copy-done.1) | copy-start | bytes 589828
  671.2 44.0 %copy-start.34 = (f32[128,768]{1,0:T(8,128)S(1)}, f32[128,768]{1,0:T(8,128)}, u32[]{:S(2)}) copy-start(f32[128,768]{1,0:T(8,128)} %copy-done.32) | copy-start | bytes 1179652
  718.3 3.3 collective-permute-start.3
  732.3 22.4 %all-to-all-start.12 = ((bf16[32,1,12,768]{3,2,1,0:T(8,128)(2,1)}), bf16[32,1,12,768]{3,2,1,0:T(8,128)(2,1)}, u32[]{:S(2)}, u32[]{:S(2)}) async-start(bf16[32,1,12,768]{3,2,1,0:T(8,128)(2,1)} %bitcast.590), calls=%async_computation.12 | async-start | bytes 1572864 | tf_op jit(solution)/shard_map/all_to_all | solution.py:228
  762.4 16.1 %all-to-all-start.14 = ((bf16[2,16,12,768]{3,0,2,1:T(2,128)(2,1)}), bf16[2,16,12,768]{3,0,2,1:T(2,128)(2,1)}, u32[]{:S(2)}, u32[]{:S(2)}) async-start(bf16[2,16,12,768]{3,0,2,1:T(2,128)(2,1)} %bitcast.603), calls=%async_computation.14 | async-start | bytes 1179648 | tf_op jit(solution)/shard_map/all_to_all | solution.py:242
  766.6 59.8 %all-reduce.28.cloned.1.call-start = ((), (), s32[]{:S(2)}) async-start(), calls=%async_computation.21 | async-start | bytes 393216 | tf_op jit(solution)/shard_map/psum | solution.py:250
  788.2 86.1 %all-reduce.30.cloned.1.call-start = ((), (), s32[]{:S(2)}) async-start(), calls=%async_computation.22 | async-start | bytes 393216 | tf_op jit(solution)/shard_map/psum | solution.py:271
  832.3 133.7 %all-reduce.32.cloned.1.call-start = ((), (), s32[]{:S(2)}) async-start(), calls=%async_computation.23 | async-start | bytes 2359296 | tf_op jit(solution)/shard_map/psum | solution.py:346
  836.9 121.0 %copy-start.69 = (f32[128,768]{1,0:T(8,128)S(1)}, f32[128,768]{1,0:T(8,128)}, u32[]{:S(2)}) copy-start(f32[128,768]{1,0:T(8,128)} %copy-done.68) | copy-start | bytes 1179652
  (226 other events, 1936.1 us)
Sparse Core Ops, SparseCore 0:
  16.6 44.6 all-reduce.15
  128.0 38.8 all-reduce.17
  176.7 42.7 all-reduce.19
  321.1 43.5 all-reduce.35
  386.0 42.1 all-reduce.23
  437.5 44.0 all-reduce.21
  614.3 42.9 all-reduce.33
  671.3 42.0 all-reduce.25
  788.3 38.0 all-reduce.27
  832.4 41.8 all-reduce.29
  878.3 87.6 all-reduce.31
